TPU v7x, 32 devices: a whole 2x2x4 slice. The times are simulated.
32 devices in a mesh: runs: 2 (over x), space: 16 (over z, y, core).
Axes of the slice: x: 2, y: 2, z: 4, core: 2. Of those that a mesh axis runs over, the one named last changes fastest.
Arguments:
- tangent: float32 [1024, 256, 128], P('runs', 'space'), parts along dimension 0, may hold values from -400 to 400
- courant_x: float32 [512, 128], P(('runs', 'space')), parts along dimension 0, may hold values from -0.4 to 0.4
- courant_y: float32 [512, 128], P(('runs', 'space')), parts along dimension 0, may hold values from -0.4 to 0.4
Outputs:
- basis: float32 [1024, 256, 128], P('runs', 'space'), parts along dimension 0
- growth: float32 [1024, 512], P('runs'), parts along dimension 0
- log_growth: float32 [1024], P('runs'), parts along dimension 0
- first_factor: float32 [1024, 512], P('runs'), parts along dimension 0
There are 2 independent parts, one for each index of `runs`. A program takes and returns all parts, laid end to end along the dimension named above; each array names one. Nothing has to cross between parts.
All inputs are finite; a program needn't handle non-finite values.
Results may differ from a plain program's by a relative error of at most 0.0012.
Values sent between devices are 32-bit elements; how exact they have to be, the bound alone decides.
A program may use at most 128 MiB of HBM per device.

v0:
```python
import jax
import jax.numpy as jnp
from jax import lax
from jax.sharding import PartitionSpec as P

diffusion_number = 0.2


def extended(cells, sides, width):
    for axis, dim in sides:
        count = lax.axis_size(axis)
        head = lax.slice_in_dim(cells, 0, width, axis=dim)
        tail = lax.slice_in_dim(cells, cells.shape[dim] - width, cells.shape[dim], axis=dim)
        cells = jnp.concatenate(
            [
                lax.ppermute(tail, axis, [(i, (i + 1) % count) for i in range(count)]),
                cells,
                lax.ppermute(head, axis, [((i + 1) % count, i) for i in range(count)]),
            ],
            axis=dim,
        )
    return cells


def update(center, east_side, west_side, courant_x, courant_y):
    north_side = jnp.roll(center, -1, 2)
    south_side = jnp.roll(center, 1, 2)
    spread = east_side + west_side + north_side + south_side - 4.0 * center
    return (
        center
        + diffusion_number * spread
        - 0.5 * courant_x * (east_side - west_side)
        - 0.5 * courant_y * (north_side - south_side)
    )


def single_step(field, courant_x, courant_y):
    padded = extended(field, (("space", 1),), 1)
    return update(padded[:, 1:-1], padded[:, 2:], padded[:, :-2], courant_x, courant_y)


def factorize(gram, flattened):
    lower = jnp.linalg.cholesky(gram)
    identity = jnp.eye(gram.shape[0], dtype=jnp.float32)
    inverse = lax.linalg.triangular_solve(lower, identity, left_side=True, lower=True)
    return (lower, jnp.dot(inverse, flattened, precision=lax.Precision.HIGHEST))


def body(tangent, courant_x, courant_y):
    advanced = single_step(single_step(tangent, courant_x, courant_y), courant_x, courant_y)
    vectors = advanced.shape[0]
    flattened = advanced.reshape(vectors, advanced.shape[1] * advanced.shape[2])
    cells = advanced.shape[1] * advanced.shape[2] * lax.axis_size("space")
    first_part = jnp.dot(flattened, flattened.T, precision=lax.Precision.HIGHEST)
    first_gram = lax.psum(first_part, "space") / cells
    first_lower, first_basis = factorize(first_gram, flattened)
    second_part = jnp.dot(first_basis, first_basis.T, precision=lax.Precision.HIGHEST)
    second_gram = lax.psum(second_part, "space") / cells
    second_lower, final_basis = factorize(second_gram, first_basis)
    growth = jnp.dot(first_lower, second_lower, precision=lax.Precision.HIGHEST).T
    log_growth = jnp.log(jnp.diagonal(first_lower)) + jnp.log(jnp.diagonal(second_lower))
    return (final_basis.reshape(advanced.shape), growth, log_growth, first_lower.T)


def solution(mesh):
    return jax.shard_map(
        body,
        mesh=mesh,
        in_specs=(P("runs", "space", None), P(("runs", "space"), None), P(("runs", "space"), None)),
        out_specs=(P("runs", "space", None), P("runs", None), P("runs"), P("runs", None)),
        check_vma=False,
    )
```

profile of v0, /device:TPU:0, one launch (start us, length us, event | category | flops | bytes accessed | tf_op | source)
XLA Modules:
  0.0 612.8 jit_solution(12937679501652068149)
XLA Ops:
  7.2 2.6 fusion.97
  9.8 5.5 collective-permute-start
  15.3 5.2 copy.47
  20.5 8.2 %fusion.98 = (f32[512,16,127]{0,2,1:T(8,128)}, f32[512,16,127]{0,2,1:T(8,128)}) fusion(f32[512,16,128]{0,2,1:T(8,128)} %copy.47), kind=kLoop, calls=%fused_computation.177 | loop fusion | bytes 16646144 | tf_op jit(solution)/shard_map/jit(_roll_static)/slice | solution.py:26
  30.1 9.0 %multiply_subtract_fusion.1 = f32[512,16,128]{0,2,1:T(8,128)S(1)} fusion(f32[512,16,128]{0,2,1:T(8,128)} %copy.47, f32[512,16,127]{0,2,1:T(8,128)} %get-tuple-element.71, f32[512,16,1]{0,2,1:T(1,128)S(1)} %get-tuple-element.73, f32[512,16,1]{0,2,1:T(1,128)S(1)} %get-tuple-element.72, f32[512,16,127]{0,2,1:T(8,128)} %get-tuple-element.70, ...), kind=kLoop, calls=%fused_computation.15 | loop fusion | flops 17825792 | bytes 17317888 | tf_op jit(solution)/shard_map/sub | solution.py:30
  39.1 2.0 copy-done.2
  41.3 4.5 collective-permute-start.2
  46.5 8.2 %fusion.95 = (f32[512,16,127]{0,2,1:T(8,128)}, f32[512,16,127]{0,2,1:T(8,128)}) fusion(f32[512,16,128]{0,2,1:T(8,128)} %copy-done.2), kind=kLoop, calls=%fused_computation.174 | loop fusion | bytes 16646144 | tf_op jit(solution)/shard_map/jit(_roll_static)/slice | solution.py:26
  56.0 9.0 %multiply_subtract_fusion = f32[512,16,128]{0,2,1:T(8,128)S(1)} fusion(f32[512,16,128]{0,2,1:T(8,128)} %copy-done.2, f32[512,16,127]{0,2,1:T(8,128)} %get-tuple-element.65, f32[512,16,1]{0,2,1:T(1,128)S(1)} %get-tuple-element.67, f32[512,16,1]{0,2,1:T(1,128)S(1)} %get-tuple-element.66, f32[512,16,127]{0,2,1:T(8,128)} %get-tuple-element.64, ...), kind=kLoop, calls=%fused_computation.14 | loop fusion | flops 17825792 | bytes 17317888 | tf_op jit(solution)/shard_map/sub | solution.py:30
  65.0 2.0 copy-done.3
  67.0 8.0 %convolution_bitcast_fusion.1 = f32[512,512]{0,1:T(8,128)} fusion(f32[512,16,128]{0,2,1:T(8,128)S(1)} %multiply_subtract_fusion), kind=kOutput, calls=%fused_computation.17 | convolution fusion | flops 6442450944 | bytes 5242880 | tf_op jit(solution)/shard_map/dot_general | solution.py:54
  75.5 94.1 %all-reduce.4.cloned.1.call-done = f32[512,512]{0,1:T(8,128)} async-done(((f32[512,512]{0,1:T(8,128)}), f32[512,512]{0,1:T(8,128)}) %all-reduce.4.cloned.1.call-update) | async-done | bytes 1048592 | tf_op jit(solution)/shard_map/psum | solution.py:55
  169.6 2.4 broadcast_multiply_fusion.1
  171.9 1.6 copy.55
  174.7 11.7 %cholesky.286 = f32[128,128]{1,0:T(8,128)S(1)} custom-call(f32[128,128]{1,0:T(8,128)S(1)} %cholesky.426), custom_call_target="Cholesky" | custom-call | tf_op jit(solution)/shard_map/jit(cholesky)/cholesky | solution.py:43
  186.6 9.8 %custom-call.31 = f32[1,128,128]{1,2,0:T(8,128)S(1)} custom-call(f32[1,128,128]{2,1,0:T(8,128)S(1)} %get-tuple-element.93), custom_call_target="InvertDiagBlocksLowerTriangular" | custom-call | tf_op jit(solution)/shard_map/jit(cholesky)/cholesky | solution.py:43
  197.7 1.3 convolution_subtract_fusion.7
  199.0 11.7 %cholesky.305 = f32[128,128]{1,0:T(8,128)S(1)} custom-call(f32[128,128]{1,0:T(8,128)S(1)} %cholesky.430), custom_call_target="Cholesky" | custom-call | tf_op jit(solution)/shard_map/jit(cholesky)/cholesky | solution.py:43
  212.1 10.2 %custom-call.32 = f32[1,128,128]{1,2,0:T(8,128)S(1)} custom-call(f32[1,128,128]{2,1,0:T(8,128)S(1)} %get-tuple-element.90), custom_call_target="InvertDiagBlocksLowerTriangular" | custom-call | tf_op jit(solution)/shard_map/jit(cholesky)/cholesky | solution.py:43
  222.5 1.3 convolution_subtract_fusion.9
  223.8 11.7 %cholesky.326 = f32[128,128]{1,0:T(8,128)S(1)} custom-call(f32[128,128]{1,0:T(8,128)S(1)} %cholesky.435), custom_call_target="Cholesky" | custom-call | tf_op jit(solution)/shard_map/jit(cholesky)/cholesky | solution.py:43
  236.2 9.8 %custom-call.33 = f32[1,128,128]{1,2,0:T(8,128)S(1)} custom-call(f32[1,128,128]{2,1,0:T(8,128)S(1)} %get-tuple-element.87), custom_call_target="InvertDiagBlocksLowerTriangular" | custom-call | tf_op jit(solution)/shard_map/jit(cholesky)/cholesky | solution.py:43
  247.5 11.9 %cholesky.343 = f32[128,128]{1,0:T(8,128)S(1)} custom-call(f32[128,128]{1,0:T(8,128)S(1)} %convolution_subtract_fusion.11), custom_call_target="Cholesky" | custom-call | tf_op jit(solution)/shard_map/jit(cholesky)/cholesky | solution.py:43
  263.8 11.7 %while.4 = (s32[]{:T(128)}, f32[512,512]{1,0:T(8,128)}, s32[4,2]{0,1:T(2,128)S(1)}, f32[4,128,128]{2,1,0:T(8,128)S(1)}, s32[]{:T(128)}) while((s32[]{:T(128)}, f32[512,512]{1,0:T(8,128)}, s32[4,2]{0,1:T(2,128)S(1)}, f32[4,128,128]{2,1,0:T(8,128)S(1)}, s32[]{:T(128)}) %tuple.67), condition=%wide.while_cond, body=%wide.while_body.sunk | while | flops 2 | bytes 131181 | solution.py:45
  264.5 2.2 bitcast_dynamic-update-slice_fusion.4
  267.5 2.2 bitcast_dynamic-update-slice_fusion.4
  270.4 2.2 bitcast_dynamic-update-slice_fusion.4
  273.3 2.2 bitcast_dynamic-update-slice_fusion.4
  275.5 39.3 %custom-call.34 = f32[4,128,128]{1,2,0:T(8,128)S(1)} custom-call(f32[4,128,128]{2,1,0:T(8,128)S(1)} %get-tuple-element.20), custom_call_target="InvertDiagBlocksLowerTriangular" | custom-call | tf_op jit(solution)/shard_map/triangular_solve/custom-call.3 | solution.py:45
  315.3 1.4 convolution_subtract_fusion.3
  317.2 1.3 convolution_subtract_fusion.2
  318.9 1.6 convolution_subtract_fusion.5
  320.9 7.1 %fusion = f32[512,2048]{1,0:T(8,128)S(1)} fusion(f32[512,2048]{0,1:T(8,128)S(1)} %bitcast.116, f32[128,512]{1,0:T(8,128)S(1)} %fusion.64, f32[128,512]{1,0:T(8,128)S(1)} %fusion.65, f32[128,512]{1,0:T(8,128)S(1)} %fusion.67, f32[128,512]{1,0:T(8,128)S(1)} %fusion.42), kind=kOutput, calls=%fused_computation.34 | convolution fusion | flops 6443237376 | bytes 9437184 | tf_op jit(solution)/shard_map/dot_general | solution.py:46
  328.1 2.0 copy-done
  330.1 8.3 %fusion.100 = f32[512,512]{0,1:T(8,128)} fusion(f32[512,2048]{1,0:T(8,128)S(1)} %fusion), kind=kOutput, calls=%fused_computation.179 | convolution fusion | flops 6442450944 | bytes 5242880 | tf_op jit(solution)/shard_map/dot_general | solution.py:57
  338.4 4.5 gather_fusion
  343.0 1.3 copy.58
  344.3 86.7 %all-reduce.6.cloned.1.call-done = f32[512,512]{0,1:T(8,128)} async-done(((f32[512,512]{0,1:T(8,128)}), f32[512,512]{0,1:T(8,128)}) %all-reduce.6.cloned.1.call-update) | async-done | bytes 1048592 | tf_op jit(solution)/shard_map/psum | solution.py:58
  431.0 2.4 broadcast_multiply_fusion
  433.4 2.6 copy.57
  436.0 1.5 fusion.15
  438.4 11.7 %cholesky.358 = f32[128,128]{1,0:T(8,128)S(1)} custom-call(f32[128,128]{1,0:T(8,128)S(1)} %cholesky.439), custom_call_target="Cholesky" | custom-call | tf_op jit(solution)/shard_map/jit(cholesky)/cholesky | solution.py:43
  450.3 9.8 %custom-call.35 = f32[1,128,128]{1,2,0:T(8,128)S(1)} custom-call(f32[1,128,128]{2,1,0:T(8,128)S(1)} %get-tuple-element.83), custom_call_target="InvertDiagBlocksLowerTriangular" | custom-call | tf_op jit(solution)/shard_map/jit(cholesky)/cholesky | solution.py:43
  461.4 1.3 convolution_subtract_fusion.6
  462.6 11.7 %cholesky.377 = f32[128,128]{1,0:T(8,128)S(1)} custom-call(f32[128,128]{1,0:T(8,128)S(1)} %cholesky.443), custom_call_target="Cholesky" | custom-call | tf_op jit(solution)/shard_map/jit(cholesky)/cholesky | solution.py:43
  475.7 10.0 %custom-call.36 = f32[1,128,128]{1,2,0:T(8,128)S(1)} custom-call(f32[1,128,128]{2,1,0:T(8,128)S(1)} %get-tuple-element.80), custom_call_target="InvertDiagBlocksLowerTriangular" | custom-call | tf_op jit(solution)/shard_map/jit(cholesky)/cholesky | solution.py:43
  486.0 1.3 convolution_subtract_fusion.8
  487.3 11.7 %cholesky.398 = f32[128,128]{1,0:T(8,128)S(1)} custom-call(f32[128,128]{1,0:T(8,128)S(1)} %cholesky.448), custom_call_target="Cholesky" | custom-call | tf_op jit(solution)/shard_map/jit(cholesky)/cholesky | solution.py:43
  499.7 9.8 %custom-call.37 = f32[1,128,128]{1,2,0:T(8,128)S(1)} custom-call(f32[1,128,128]{2,1,0:T(8,128)S(1)} %get-tuple-element.77), custom_call_target="InvertDiagBlocksLowerTriangular" | custom-call | tf_op jit(solution)/shard_map/jit(cholesky)/cholesky | solution.py:43
  511.0 11.9 %cholesky.415 = f32[128,128]{1,0:T(8,128)S(1)} custom-call(f32[128,128]{1,0:T(8,128)S(1)} %convolution_subtract_fusion.10), custom_call_target="Cholesky" | custom-call | tf_op jit(solution)/shard_map/jit(cholesky)/cholesky | solution.py:43
  526.2 2.4 fusion.20
  528.6 4.5 gather_fusion.1
  533.1 4.5 fusion.101
  537.7 11.7 %while.5 = (s32[]{:T(128)}, f32[512,512]{1,0:T(8,128)}, s32[4,2]{0,1:T(2,128)S(1)}, f32[4,128,128]{2,1,0:T(8,128)S(1)}, s32[]{:T(128)}) while((s32[]{:T(128)}, f32[512,512]{1,0:T(8,128)}, s32[4,2]{0,1:T(2,128)S(1)}, f32[4,128,128]{2,1,0:T(8,128)S(1)}, s32[]{:T(128)}) %tuple.77), condition=%wide.while_cond.clone, body=%wide.while_body.clone.sunk | while | flops 2 | bytes 131181 | solution.py:45
  538.4 2.3 bitcast_dynamic-update-slice_fusion.5
  541.3 2.3 bitcast_dynamic-update-slice_fusion.5
  544.3 2.3 bitcast_dynamic-update-slice_fusion.5
  547.2 2.2 bitcast_dynamic-update-slice_fusion.5
  549.4 39.6 %custom-call.38 = f32[4,128,128]{1,2,0:T(8,128)S(1)} custom-call(f32[4,128,128]{2,1,0:T(8,128)S(1)} %get-tuple-element.21), custom_call_target="InvertDiagBlocksLowerTriangular" | custom-call | tf_op jit(solution)/shard_map/triangular_solve/custom-call.3 | solution.py:45
  589.4 1.4 convolution_subtract_fusion.1
  591.3 1.3 convolution_subtract_fusion
  593.0 1.6 convolution_subtract_fusion.4
  595.0 7.1 %convolution_bitcast_fusion = f32[64,8,16,128]{3,1,2,0:T(8,128)S(1)} fusion(f32[512,2048]{1,0:T(8,128)S(1)} %copy-done.1, f32[128,512]{1,0:T(8,128)S(1)} %fusion.58, f32[128,512]{1,0:T(8,128)S(1)} %fusion.59, f32[128,512]{1,0:T(8,128)S(1)} %fusion.61, f32[128,512]{1,0:T(8,128)S(1)} %fusion.40), kind=kOutput, calls=%fused_computation.16 | convolution fusion | flops 6443237376 | bytes 9437184 | tf_op jit(solution)/shard_map/dot_general | solution.py:46
  602.2 2.9 copy.66
  (106 shorter events, 28.6 us)
Async XLA Ops:
  7.2 162.4 %all-reduce.4.cloned.1.call-start = ((), (), s32[]{:S(2)}) async-start(), calls=%async_computation | async-start | bytes 2097152 | tf_op jit(solution)/shard_map/psum | solution.py:55
  9.8 20.1 %collective-permute-start = (f32[512,1,128]{2,0,1:T(8,128)S(1)}, f32[512,1,128]{2,0,1:T(8,128)S(1)}, u32[]{:S(2)}, u32[]{:S(2)}) collective-permute-start(f32[512,1,128]{2,0,1:T(8,128)S(1)} %bitcast.120), channel_id=1, source_target_pairs={{1,0},{2,1},{3,2},{4,3},{5,4},{6,5},{7,6},{8,7},{9,8},{10,9},{11,1... | collective-permute-start | bytes 786440 | tf_op jit(solution)/shard_map/ppermute | solution.py:18
  15.3 14.7 %collective-permute-start.1 = (f32[512,1,128]{2,0,1:T(8,128)S(1)}, f32[512,1,128]{2,0,1:T(8,128)S(1)}, u32[]{:S(2)}, u32[]{:S(2)}) collective-permute-start(f32[512,1,128]{2,0,1:T(8,128)S(1)} %bitcast.119), channel_id=1, source_target_pairs={{0,1},{1,2},{2,3},{3,4},{4,5},{5,6},{6,7},{7,8},{8,9},{9,10},{10,1... | collective-permute-start | bytes 786440 | tf_op jit(solution)/shard_map/ppermute | solution.py:16
  20.5 8.2 %copy-start.10 = (f32[16,128]{1,0:T(8,128)S(1)}, f32[16,128]{1,0:T(8,128)}, u32[]{:S(2)}) copy-start(f32[16,128]{1,0:T(8,128)} %param.8) | copy-start | bytes 24580
  20.5 8.2 %copy-start.11 = (f32[16,128]{1,0:T(8,128)S(1)}, f32[16,128]{1,0:T(8,128)}, u32[]{:S(2)}) copy-start(f32[16,128]{1,0:T(8,128)} %param.7) | copy-start | bytes 24580
  39.1 2.0 copy-start.2
  41.3 14.4 %collective-permute-start.2 = (f32[512,1,128]{2,0,1:T(8,128)S(1)}, f32[512,1,128]{2,0,1:T(8,128)S(1)}, u32[]{:S(2)}, u32[]{:S(2)}) collective-permute-start(f32[512,1,128]{2,0,1:T(8,128)S(1)} %copy.48), channel_id=1, source_target_pairs={{1,0},{2,1},{3,2},{4,3},{5,4},{6,5},{7,6},{8,7},{9,8},{10,9},{11,1... | collective-permute-start | bytes 786440 | tf_op jit(solution)/shard_map/ppermute | solution.py:18
  45.9 10.0 %collective-permute-start.3 = (f32[512,1,128]{2,0,1:T(8,128)S(1)}, f32[512,1,128]{2,0,1:T(8,128)S(1)}, u32[]{:S(2)}, u32[]{:S(2)}) collective-permute-start(f32[512,1,128]{2,0,1:T(8,128)S(1)} %copy.50), channel_id=1, source_target_pairs={{0,1},{1,2},{2,3},{3,4},{4,5},{5,6},{6,7},{7,8},{8,9},{9,10},{10,1... | collective-permute-start | bytes 786440 | tf_op jit(solution)/shard_map/ppermute | solution.py:16
  65.0 2.0 copy-start.3
  75.1 355.9 %all-reduce.6.cloned.1.call-start = ((), (), s32[]{:S(2)}) async-start(), calls=%async_computation.1 | async-start | bytes 2097152 | tf_op jit(solution)/shard_map/psum | solution.py:58
  169.6 3.9 copy-start.6
  173.8 1.0 copy-start.8
  314.9 6.1 copy-start.4
  328.1 2.0 copy-start
  431.0 5.0 copy-start.7
  437.4 1.0 copy-start.9
  522.9 3.3 copy-start.5
  589.0 6.1 copy-start.1
Sparse Core Ops, SparseCore 0:
  75.2 94.2 all-reduce.3
  338.6 92.3 all-reduce.5
where the time goes:
time: 618 us; the launch traced here: 613 us
  other arithmetic  267 us (43%)
  waiting for transfers between devices  181 us (29%)
  local copies, waits for them, and re-layouts  76.2 us (12%)
  matrix products  58.1 us (9%)
  between operations  20 us (3%)
  starting transfers between devices  10.8 us (2%)
    another operation x30, other arithmetic, factorize(): lower = jnp.linalg.cholesky(gram)  159 us
    psum x1, waiting for transfers between devices, body(): first_gram = lax.psum(first_part, 'space') / cells  94.1 us
    psum x1, waiting for transfers between devices, body(): second_gram = lax.psum(second_part, 'space') / cells  86.7 us
    another operation x5, other arithmetic, factorize(): lax.linalg.triangular_solve(lower, identity, left_side=True, lower=True)  82.5 us
    another operation x27, local copies, waits for them, and re-layouts, factorize(): lax.linalg.triangular_solve(lower, identity, left_side=True, lower=True)  23.3 us
    slice x4, local copies, waits for them, and re-layouts, update(): north_side = jnp.roll(center, -1, 2)  18.6 us
    sub x2, other arithmetic, update(): center + diffusion_number * spread  17.9 us
    unnamed x27, local copies, waits for them, and re-layouts  17.4 us
  transfers between devices with their start and end apart: 6, of which 2 were waited for; matrix products, arithmetic and copies ran while one was open for 5% of the time, Pallas kernels for 0%

commit v1 on v0

--- a/solution.py
+++ b/solution.py
@@ -55,7 +55,7 @@
     first_gram = lax.psum(first_part, "space") / cells
     first_lower, first_basis = factorize(first_gram, flattened)
     second_part = jnp.dot(first_basis, first_basis.T, precision=lax.Precision.HIGHEST)
-    second_gram = lax.psum(second_part, "space") / cells
+    second_gram = jnp.sum(lax.all_gather(second_part, "space"), axis=0) / cells
     second_lower, final_basis = factorize(second_gram, first_basis)
     growth = jnp.dot(first_lower, second_lower, precision=lax.Precision.HIGHEST).T
     log_growth = jnp.log(jnp.diagonal(first_lower)) + jnp.log(jnp.diagonal(second_lower))

time: 618 us -> 661 us (1.070)
  waiting for transfers between devices: 181 us -> 215 us
  other arithmetic: 267 us -> 274 us
    all_gather x0 -> x1, waiting for transfers between devices: none -> 120 us  [body(): second_gram = jnp.sum(lax.all_gather(second_part, 'space'), axis=0) / cells]
    psum x1 -> x0, waiting for transfers between devices: 86.7 us -> none  [body(): second_gram = lax.psum(second_part, 'space') / cells]
    reduce_sum x0 -> x1, other arithmetic: none -> 8.88 us  [body(): second_gram = jnp.sum(lax.all_gather(second_part, 'space'), axis=0) / cells]
    unnamed x27 -> x25, local copies, waits for them, and re-layouts: 17.4 us -> 17.4 us
where the time goes in v1:
time: 661 us; the launch traced here: 656 us
  other arithmetic  274 us (41%)
  waiting for transfers between devices  215 us (33%)
  local copies, waits for them, and re-layouts  77.7 us (12%)
  matrix products  58.1 us (9%)
  between operations  20.2 us (3%)
  starting transfers between devices  10.8 us (2%)
    another operation x30, other arithmetic, factorize(): lower = jnp.linalg.cholesky(gram)  159 us
    all_gather x1, waiting for transfers between devices, body(): second_gram = jnp.sum(lax.all_gather(second_part, 'space'), axis=0) / cells  120 us
    psum x1, waiting for transfers between devices, body(): first_gram = lax.psum(first_part, 'space') / cells  94.1 us
    another operation x5, other arithmetic, factorize(): lax.linalg.triangular_solve(lower, identity, left_side=True, lower=True)  82.5 us
    another operation x27, local copies, waits for them, and re-layouts, factorize(): lax.linalg.triangular_solve(lower, identity, left_side=True, lower=True)  23.3 us
    slice x4, local copies, waits for them, and re-layouts, update(): north_side = jnp.roll(center, -1, 2)  18.6 us
    sub x2, other arithmetic, update(): center + diffusion_number * spread  17.8 us
    unnamed x25, local copies, waits for them, and re-layouts  17.4 us
  transfers between devices with their start and end apart: 6, of which 2 were waited for; matrix products, arithmetic and copies ran while one was open for 5% of the time, Pallas kernels for 0%

profile of v1, /device:TPU:0, one launch (start us, length us, event | category | flops | bytes accessed | tf_op | source)
XLA Modules:
  0.0 655.8 jit_solution(18420453702416157275)
XLA Ops:
  7.2 2.6 fusion.97
  9.8 5.5 collective-permute-start
  15.3 5.2 copy.45
  20.5 8.2 %fusion.98 = (f32[512,16,127]{0,2,1:T(8,128)}, f32[512,16,127]{0,2,1:T(8,128)}) fusion(f32[512,16,128]{0,2,1:T(8,128)} %copy.45), kind=kLoop, calls=%fused_computation.177 | loop fusion | bytes 16646144 | tf_op jit(solution)/shard_map/jit(_roll_static)/slice | solution.py:26
  30.1 8.9 %multiply_subtract_fusion.1 = f32[512,16,128]{0,2,1:T(8,128)S(1)} fusion(f32[512,16,128]{0,2,1:T(8,128)} %copy.45, f32[512,16,127]{0,2,1:T(8,128)} %get-tuple-element.71, f32[512,16,1]{0,2,1:T(1,128)S(1)} %get-tuple-element.73, f32[512,16,1]{0,2,1:T(1,128)S(1)} %get-tuple-element.72, f32[512,16,127]{0,2,1:T(8,128)} %get-tuple-element.70, ...), kind=kLoop, calls=%fused_computation.15 | loop fusion | flops 17825792 | bytes 17317888 | tf_op jit(solution)/shard_map/sub | solution.py:30
  39.0 2.0 copy-done.2
  41.2 4.5 collective-permute-start.2
  46.4 8.2 %fusion.95 = (f32[512,16,127]{0,2,1:T(8,128)}, f32[512,16,127]{0,2,1:T(8,128)}) fusion(f32[512,16,128]{0,2,1:T(8,128)} %copy-done.2), kind=kLoop, calls=%fused_computation.174 | loop fusion | bytes 16646144 | tf_op jit(solution)/shard_map/jit(_roll_static)/slice | solution.py:26
  56.0 8.9 %multiply_subtract_fusion = f32[512,16,128]{0,2,1:T(8,128)S(1)} fusion(f32[512,16,128]{0,2,1:T(8,128)} %copy-done.2, f32[512,16,127]{0,2,1:T(8,128)} %get-tuple-element.65, f32[512,16,1]{0,2,1:T(1,128)S(1)} %get-tuple-element.67, f32[512,16,1]{0,2,1:T(1,128)S(1)} %get-tuple-element.66, f32[512,16,127]{0,2,1:T(8,128)} %get-tuple-element.64, ...), kind=kLoop, calls=%fused_computation.14 | loop fusion | flops 17825792 | bytes 17317888 | tf_op jit(solution)/shard_map/sub | solution.py:30
  64.9 2.0 copy-done.3
  66.9 8.0 %convolution_bitcast_fusion.1 = f32[512,512]{0,1:T(8,128)} fusion(f32[512,16,128]{0,2,1:T(8,128)S(1)} %multiply_subtract_fusion), kind=kOutput, calls=%fused_computation.17 | convolution fusion | flops 6442450944 | bytes 5242880 | tf_op jit(solution)/shard_map/dot_general | solution.py:54
  75.3 94.1 %all-reduce.3.cloned.1.call-done = f32[512,512]{0,1:T(8,128)} async-done(((f32[512,512]{0,1:T(8,128)}), f32[512,512]{0,1:T(8,128)}) %all-reduce.3.cloned.1.call-update) | async-done | bytes 1048592 | tf_op jit(solution)/shard_map/psum | solution.py:55
  169.4 2.4 broadcast_multiply_fusion.1
  171.8 1.6 copy.53
  174.6 11.7 %cholesky.286 = f32[128,128]{1,0:T(8,128)S(1)} custom-call(f32[128,128]{1,0:T(8,128)S(1)} %cholesky.426), custom_call_target="Cholesky" | custom-call | tf_op jit(solution)/shard_map/jit(cholesky)/cholesky | solution.py:43
  186.5 9.8 %custom-call.31 = f32[1,128,128]{1,2,0:T(8,128)S(1)} custom-call(f32[1,128,128]{2,1,0:T(8,128)S(1)} %get-tuple-element.93), custom_call_target="InvertDiagBlocksLowerTriangular" | custom-call | tf_op jit(solution)/shard_map/jit(cholesky)/cholesky | solution.py:43
  197.5 1.3 convolution_subtract_fusion.7
  198.8 11.7 %cholesky.305 = f32[128,128]{1,0:T(8,128)S(1)} custom-call(f32[128,128]{1,0:T(8,128)S(1)} %cholesky.430), custom_call_target="Cholesky" | custom-call | tf_op jit(solution)/shard_map/jit(cholesky)/cholesky | solution.py:43
  211.9 10.2 %custom-call.32 = f32[1,128,128]{1,2,0:T(8,128)S(1)} custom-call(f32[1,128,128]{2,1,0:T(8,128)S(1)} %get-tuple-element.90), custom_call_target="InvertDiagBlocksLowerTriangular" | custom-call | tf_op jit(solution)/shard_map/jit(cholesky)/cholesky | solution.py:43
  222.4 1.3 convolution_subtract_fusion.9
  223.7 11.7 %cholesky.326 = f32[128,128]{1,0:T(8,128)S(1)} custom-call(f32[128,128]{1,0:T(8,128)S(1)} %cholesky.435), custom_call_target="Cholesky" | custom-call | tf_op jit(solution)/shard_map/jit(cholesky)/cholesky | solution.py:43
  236.1 9.8 %custom-call.33 = f32[1,128,128]{1,2,0:T(8,128)S(1)} custom-call(f32[1,128,128]{2,1,0:T(8,128)S(1)} %get-tuple-element.87), custom_call_target="InvertDiagBlocksLowerTriangular" | custom-call | tf_op jit(solution)/shard_map/jit(cholesky)/cholesky | solution.py:43
  247.4 11.9 %cholesky.343 = f32[128,128]{1,0:T(8,128)S(1)} custom-call(f32[128,128]{1,0:T(8,128)S(1)} %convolution_subtract_fusion.11), custom_call_target="Cholesky" | custom-call | tf_op jit(solution)/shard_map/jit(cholesky)/cholesky | solution.py:43
  263.7 11.7 %while.4 = (s32[]{:T(128)}, f32[512,512]{1,0:T(8,128)}, s32[4,2]{0,1:T(2,128)S(1)}, f32[4,128,128]{2,1,0:T(8,128)S(1)}, s32[]{:T(128)}) while((s32[]{:T(128)}, f32[512,512]{1,0:T(8,128)}, s32[4,2]{0,1:T(2,128)S(1)}, f32[4,128,128]{2,1,0:T(8,128)S(1)}, s32[]{:T(128)}) %tuple.67), condition=%wide.while_cond, body=%wide.while_body.sunk | while | flops 2 | bytes 131181 | solution.py:45
  264.4 2.2 bitcast_dynamic-update-slice_fusion.4
  267.3 2.2 bitcast_dynamic-update-slice_fusion.4
  270.3 2.2 bitcast_dynamic-update-slice_fusion.4
  273.2 2.2 bitcast_dynamic-update-slice_fusion.4
  275.4 39.3 %custom-call.34 = f32[4,128,128]{1,2,0:T(8,128)S(1)} custom-call(f32[4,128,128]{2,1,0:T(8,128)S(1)} %get-tuple-element.20), custom_call_target="InvertDiagBlocksLowerTriangular" | custom-call | tf_op jit(solution)/shard_map/triangular_solve/custom-call.3 | solution.py:45
  315.2 1.4 convolution_subtract_fusion.3
  317.0 1.3 convolution_subtract_fusion.2
  318.8 1.6 convolution_subtract_fusion.5
  320.8 7.1 %fusion = f32[512,2048]{1,0:T(8,128)S(1)} fusion(f32[512,2048]{0,1:T(8,128)S(1)} %bitcast.117, f32[128,512]{1,0:T(8,128)S(1)} %fusion.64, f32[128,512]{1,0:T(8,128)S(1)} %fusion.65, f32[128,512]{1,0:T(8,128)S(1)} %fusion.67, f32[128,512]{1,0:T(8,128)S(1)} %fusion.42), kind=kOutput, calls=%fused_computation.34 | convolution fusion | flops 6443237376 | bytes 9437184 | tf_op jit(solution)/shard_map/dot_general | solution.py:46
  328.0 2.0 copy-done
  330.0 8.3 %fusion.100 = f32[512,512]{1,0:T(8,128)} fusion(f32[512,2048]{1,0:T(8,128)S(1)} %fusion), kind=kOutput, calls=%fused_computation.179 | convolution fusion | flops 6442450944 | bytes 5242880 | tf_op jit(solution)/shard_map/dot_general | solution.py:57
  338.3 4.5 gather_fusion
  342.8 1.3 copy.56
  344.2 120.4 %all-gather.3.cloned.1.call-done = f32[8192,512]{1,0:T(8,128)} async-done(((f32[512,512]{1,0:T(8,128)}), f32[8192,512]{1,0:T(8,128)}) %all-gather.3.cloned.1.call-update) | async-done | bytes 16777232 | tf_op jit(solution)/shard_map/all_gather | solution.py:58
  464.6 8.9 %reduce_sum.9 = f32[512,512]{1,0:T(8,128)} reduce(f32[16,512,512]{2,1,0:T(8,128)} %bitcast.119, f32[]{:T(128)} %constant.119.clone.1), dimensions={0}, to_apply=%region_9.12 | reduce | flops 3932160 | bytes 17825796 | tf_op jit(solution)/shard_map/reduce_sum | solution.py:58
  473.5 1.6 copy.54
  476.1 2.5 copy.55
  478.7 1.5 fusion.15
  481.1 11.7 %cholesky.358 = f32[128,128]{1,0:T(8,128)S(1)} custom-call(f32[128,128]{1,0:T(8,128)S(1)} %cholesky.439), custom_call_target="Cholesky" | custom-call | tf_op jit(solution)/shard_map/jit(cholesky)/cholesky | solution.py:43
  493.0 9.8 %custom-call.35 = f32[1,128,128]{1,2,0:T(8,128)S(1)} custom-call(f32[1,128,128]{2,1,0:T(8,128)S(1)} %get-tuple-element.83), custom_call_target="InvertDiagBlocksLowerTriangular" | custom-call | tf_op jit(solution)/shard_map/jit(cholesky)/cholesky | solution.py:43
  505.3 11.9 %cholesky.377 = f32[128,128]{1,0:T(8,128)S(1)} custom-call(f32[128,128]{1,0:T(8,128)S(1)} %cholesky.443), custom_call_target="Cholesky" | custom-call | tf_op jit(solution)/shard_map/jit(cholesky)/cholesky | solution.py:43
  518.6 9.8 %custom-call.36 = f32[1,128,128]{1,2,0:T(8,128)S(1)} custom-call(f32[1,128,128]{2,1,0:T(8,128)S(1)} %get-tuple-element.80), custom_call_target="InvertDiagBlocksLowerTriangular" | custom-call | tf_op jit(solution)/shard_map/jit(cholesky)/cholesky | solution.py:43
  528.7 1.3 convolution_subtract_fusion.8
  530.0 11.7 %cholesky.398 = f32[128,128]{1,0:T(8,128)S(1)} custom-call(f32[128,128]{1,0:T(8,128)S(1)} %cholesky.448), custom_call_target="Cholesky" | custom-call | tf_op jit(solution)/shard_map/jit(cholesky)/cholesky | solution.py:43
  542.4 9.8 %custom-call.37 = f32[1,128,128]{1,2,0:T(8,128)S(1)} custom-call(f32[1,128,128]{2,1,0:T(8,128)S(1)} %get-tuple-element.77), custom_call_target="InvertDiagBlocksLowerTriangular" | custom-call | tf_op jit(solution)/shard_map/jit(cholesky)/cholesky | solution.py:43
  553.6 11.9 %cholesky.415 = f32[128,128]{1,0:T(8,128)S(1)} custom-call(f32[128,128]{1,0:T(8,128)S(1)} %convolution_subtract_fusion.10), custom_call_target="Cholesky" | custom-call | tf_op jit(solution)/shard_map/jit(cholesky)/cholesky | solution.py:43
  569.0 2.4 fusion.20
  571.4 4.5 gather_fusion.1
  575.9 4.5 fusion.101
  580.4 11.7 %while.5 = (s32[]{:T(128)}, f32[512,512]{1,0:T(8,128)}, s32[4,2]{0,1:T(2,128)S(1)}, f32[4,128,128]{2,1,0:T(8,128)S(1)}, s32[]{:T(128)}) while((s32[]{:T(128)}, f32[512,512]{1,0:T(8,128)}, s32[4,2]{0,1:T(2,128)S(1)}, f32[4,128,128]{2,1,0:T(8,128)S(1)}, s32[]{:T(128)}) %tuple.77), condition=%wide.while_cond.clone, body=%wide.while_body.clone.sunk | while | flops 2 | bytes 131181 | solution.py:45
  581.1 2.3 bitcast_dynamic-update-slice_fusion.5
  584.1 2.3 bitcast_dynamic-update-slice_fusion.5
  587.0 2.3 bitcast_dynamic-update-slice_fusion.5
  590.0 2.2 bitcast_dynamic-update-slice_fusion.5
  592.2 39.6 %custom-call.38 = f32[4,128,128]{1,2,0:T(8,128)S(1)} custom-call(f32[4,128,128]{2,1,0:T(8,128)S(1)} %get-tuple-element.21), custom_call_target="InvertDiagBlocksLowerTriangular" | custom-call | tf_op jit(solution)/shard_map/triangular_solve/custom-call.3 | solution.py:45
  632.2 1.4 convolution_subtract_fusion.1
  634.0 1.3 convolution_subtract_fusion
  635.8 1.6 convolution_subtract_fusion.4
  637.8 7.1 %convolution_bitcast_fusion = f32[64,8,16,128]{3,1,2,0:T(8,128)S(1)} fusion(f32[512,2048]{1,0:T(8,128)S(1)} %copy-done.1, f32[128,512]{1,0:T(8,128)S(1)} %fusion.58, f32[128,512]{1,0:T(8,128)S(1)} %fusion.59, f32[128,512]{1,0:T(8,128)S(1)} %fusion.61, f32[128,512]{1,0:T(8,128)S(1)} %fusion.40), kind=kOutput, calls=%fused_computation.16 | convolution fusion | flops 6443237376 | bytes 9437184 | tf_op jit(solution)/shard_map/dot_general | solution.py:46
  645.0 2.9 copy.63
  (106 shorter events, 31.1 us)
Async XLA Ops:
  7.2 162.3 %all-reduce.3.cloned.1.call-start = ((), (), s32[]{:S(2)}) async-start(), calls=%async_computation | async-start | bytes 2097152 | tf_op jit(solution)/shard_map/psum | solution.py:55
  9.8 20.1 %collective-permute-start = (f32[512,1,128]{2,0,1:T(8,128)S(1)}, f32[512,1,128]{2,0,1:T(8,128)S(1)}, u32[]{:S(2)}, u32[]{:S(2)}) collective-permute-start(f32[512,1,128]{2,0,1:T(8,128)S(1)} %bitcast.122), channel_id=1, source_target_pairs={{1,0},{2,1},{3,2},{4,3},{5,4},{6,5},{7,6},{8,7},{9,8},{10,9},{11,1... | collective-permute-start | bytes 786440 | tf_op jit(solution)/shard_map/ppermute | solution.py:18
  15.3 14.7 %collective-permute-start.1 = (f32[512,1,128]{2,0,1:T(8,128)S(1)}, f32[512,1,128]{2,0,1:T(8,128)S(1)}, u32[]{:S(2)}, u32[]{:S(2)}) collective-permute-start(f32[512,1,128]{2,0,1:T(8,128)S(1)} %bitcast.121), channel_id=1, source_target_pairs={{0,1},{1,2},{2,3},{3,4},{4,5},{5,6},{6,7},{7,8},{8,9},{9,10},{10,1... | collective-permute-start | bytes 786440 | tf_op jit(solution)/shard_map/ppermute | solution.py:16
  20.5 8.2 %copy-start.9 = (f32[16,128]{1,0:T(8,128)S(1)}, f32[16,128]{1,0:T(8,128)}, u32[]{:S(2)}) copy-start(f32[16,128]{1,0:T(8,128)} %param.8) | copy-start | bytes 24580
  20.5 8.2 %copy-start.10 = (f32[16,128]{1,0:T(8,128)S(1)}, f32[16,128]{1,0:T(8,128)}, u32[]{:S(2)}) copy-start(f32[16,128]{1,0:T(8,128)} %param.7) | copy-start | bytes 24580
  39.0 2.0 copy-start.2
  41.2 14.5 %collective-permute-start.2 = (f32[512,1,128]{2,0,1:T(8,128)S(1)}, f32[512,1,128]{2,0,1:T(8,128)S(1)}, u32[]{:S(2)}, u32[]{:S(2)}) collective-permute-start(f32[512,1,128]{2,0,1:T(8,128)S(1)} %copy.46), channel_id=1, source_target_pairs={{1,0},{2,1},{3,2},{4,3},{5,4},{6,5},{7,6},{8,7},{9,8},{10,9},{11,1... | collective-permute-start | bytes 786440 | tf_op jit(solution)/shard_map/ppermute | solution.py:18
  45.8 10.0 %collective-permute-start.3 = (f32[512,1,128]{2,0,1:T(8,128)S(1)}, f32[512,1,128]{2,0,1:T(8,128)S(1)}, u32[]{:S(2)}, u32[]{:S(2)}) collective-permute-start(f32[512,1,128]{2,0,1:T(8,128)S(1)} %copy.48), channel_id=1, source_target_pairs={{0,1},{1,2},{2,3},{3,4},{4,5},{5,6},{6,7},{7,8},{8,9},{9,10},{10,1... | collective-permute-start | bytes 786440 | tf_op jit(solution)/shard_map/ppermute | solution.py:16
  64.9 2.0 copy-start.3
  75.0 389.6 %all-gather.3.cloned.1.call-start = ((), (), s32[]{:S(2)}) async-start(), calls=%async_computation.1 | async-start | bytes 17825792 | tf_op jit(solution)/shard_map/all_gather | solution.py:58
  169.4 3.9 copy-start.6
  173.6 1.0 copy-start.7
  314.7 6.1 copy-start.4
  328.0 2.0 copy-start
  480.1 1.0 copy-start.8
  565.6 3.4 copy-start.5
  631.7 6.1 copy-start.1
Sparse Core Ops, SparseCore 0:
  75.1 94.2 all-reduce.2
  338.4 126.1 all-gather.2
